TPU v7x, 32 devices: a whole 2x2x4 slice. The times are simulated.
32 devices in a mesh: stn: 4 (over x, core), tm: 8 (over z, y).
Axes of the slice: x: 2, y: 2, z: 4, core: 2. Of those that a mesh axis runs over, the one named last changes fastest.
Arguments:
- samples: bfloat16 [2, 1024, 8, 20736], P(None, 'stn', 'tm'), may hold values from -22 to 22
- filter_taps: float32 [6, 3456], replicated, may hold values from -2.5 to 2.5
- station_flags: int32 [1024], P('stn'), may hold values 0 or 1
- channel_keep: int32 [3456], replicated, may hold values from 0 to 1, as said below
- beam_delay: int32 [64, 1024], replicated, may hold values from 0 to 3455
Outputs:
- visibilities: float32 [16, 2, 1024, 1024], P(None, None, 'stn', 'tm')
- beam_power: float32 [64, 3456], P('stn', 'tm')
Inputs may be any that keep to these rules, and one draw needn't show every extreme that they name: `channel_keep`: each value is 0 or 1, and the first fine channel of every output channel is 1.
All inputs are finite; a program needn't handle non-finite values. No bound on the sum of `station_flags` on one device may be relied on, other than what follows from the above.
Results may differ from a plain program's by a relative error of at most 0.013.
Values may be sent and summed in bfloat16 or wider, within the bound.
A program may use at most 128 MiB of HBM per device.

v0:
```python
import math
import jax
import jax.numpy as jnp
from jax import lax
from jax.sharding import PartitionSpec as P

INPUTS = 1024
FINE = 3456
OUTCH = 16
TAPS = 6
TRANSFORM_PRECISION = lax.Precision.HIGH


def phase_table(row_count, col_count, modulus):
    row_ids = lax.broadcasted_iota(jnp.int32, (row_count, col_count), 0)
    col_ids = lax.broadcasted_iota(jnp.int32, (row_count, col_count), 1)
    angles = (row_ids * col_ids % modulus).astype(jnp.float32) * (2.0 * math.pi / modulus)
    return (jnp.cos(angles), jnp.sin(angles))


def fine_spectra(samples, filter_taps, station_flags):
    inputs_dev = samples.shape[1]
    spec_dev = samples.shape[2]
    framed = samples.reshape(2, inputs_dev, spec_dev, TAPS, FINE)
    branch = jnp.sum(framed.astype(jnp.float32) * filter_taps[None, None, None], axis=3)
    fft_inner = 128
    fft_outer = FINE // fft_inner
    grid_view = branch.reshape(2, inputs_dev, spec_dev, fft_outer, fft_inner)
    cos_outer, sin_outer = phase_table(fft_outer, fft_outer, fft_outer)
    first_real = jnp.einsum(
        "kn,isnm->iskm", cos_outer, grid_view[0], precision=TRANSFORM_PRECISION
    ) + jnp.einsum("kn,isnm->iskm", sin_outer, grid_view[1], precision=TRANSFORM_PRECISION)
    first_imag = jnp.einsum(
        "kn,isnm->iskm", cos_outer, grid_view[1], precision=TRANSFORM_PRECISION
    ) - jnp.einsum("kn,isnm->iskm", sin_outer, grid_view[0], precision=TRANSFORM_PRECISION)
    cos_twist, sin_twist = phase_table(fft_outer, fft_inner, FINE)
    second_real = first_real * cos_twist + first_imag * sin_twist
    second_imag = first_imag * cos_twist - first_real * sin_twist
    cos_inner, sin_inner = phase_table(fft_inner, fft_inner, fft_inner)
    third_real = jnp.einsum(
        "qm,iskm->isqk", cos_inner, second_real, precision=TRANSFORM_PRECISION
    ) + jnp.einsum("qm,iskm->isqk", sin_inner, second_imag, precision=TRANSFORM_PRECISION)
    third_imag = jnp.einsum(
        "qm,iskm->isqk", cos_inner, second_imag, precision=TRANSFORM_PRECISION
    ) - jnp.einsum("qm,iskm->isqk", sin_inner, second_real, precision=TRANSFORM_PRECISION)
    factor = station_flags.astype(jnp.float32)[:, None, None] / math.sqrt(FINE)
    stacked = (
        jnp.stack(
            [
                third_real.reshape(inputs_dev, spec_dev, FINE),
                third_imag.reshape(inputs_dev, spec_dev, FINE),
            ]
        )
        * factor
    )
    return stacked.astype(jnp.bfloat16)


def beam_terms(delay_rows, incoming, fine_global):
    phase_turns = delay_rows[:, :, None] * fine_global[None, None, :] % FINE
    angles = phase_turns.astype(jnp.float32) * (2.0 * math.pi / FINE)
    weights = jnp.stack([jnp.cos(angles), jnp.sin(angles)]).astype(jnp.bfloat16)
    products = jnp.einsum("pbik,qitk->pqbtk", weights, incoming, preferred_element_type=jnp.float32)
    volt_real = products[0, 0] + products[1, 1]
    volt_imag = products[0, 1] - products[1, 0]
    return jnp.stack([volt_real, volt_imag])


def cross_products(left_data, right_data, local_count, sub_len):
    row_count = left_data.shape[1]
    col_count = right_data.shape[1]
    spec_count = left_data.shape[2]
    left_rows = left_data.reshape(2 * row_count, spec_count, local_count, sub_len)
    right_rows = right_data.reshape(2 * col_count, spec_count, local_count, sub_len)
    products = jnp.einsum(
        "atlg,btlg->lab", left_rows, right_rows, preferred_element_type=jnp.float32
    )
    vis_real = products[:, :row_count, :col_count] + products[:, row_count:, col_count:]
    vis_imag = products[:, row_count:, :col_count] - products[:, :row_count, col_count:]
    return jnp.stack([vis_real, vis_imag], axis=1)


def on_device(samples, filter_taps, station_flags, channel_keep, beam_delay):
    spectra = fine_spectra(samples, filter_taps, station_flags)
    turned = lax.all_to_all(spectra, "tm", split_axis=3, concat_axis=2, tiled=True)
    inputs_dev = turned.shape[1]
    spectra_all = turned.shape[2]
    fine_dev = turned.shape[3]
    group_len = FINE // OUTCH
    sub_len = min(group_len, fine_dev)
    local_count = fine_dev // sub_len
    tm_index = lax.axis_index("tm")
    stn_index = lax.axis_index("stn")
    fine_start = tm_index * fine_dev
    keep_local = lax.dynamic_slice_in_dim(channel_keep, fine_start, fine_dev, 0)
    keep_wide = keep_local.astype(jnp.bfloat16)
    fine_global = fine_start + jnp.arange(fine_dev, dtype=jnp.int32)
    masked = turned * keep_wide
    vis_local = cross_products(
        masked, lax.all_gather(turned, "stn", axis=1, tiled=True), local_count, sub_len
    )
    own_delays = lax.dynamic_slice_in_dim(beam_delay, stn_index * inputs_dev, inputs_dev, 1)
    voltages = lax.psum_scatter(
        beam_terms(own_delays, turned, fine_global).astype(jnp.bfloat16),
        "stn",
        scatter_dimension=1,
        tiled=True,
    ).astype(jnp.float32)
    beam_energy = jnp.sum(voltages[0] * voltages[0] + voltages[1] * voltages[1], axis=1)
    beam_power = beam_energy * keep_local.astype(jnp.float32) / (INPUTS * spectra_all)
    counts = jnp.sum(channel_keep.reshape(OUTCH, group_len), axis=1)
    first_channel = fine_start // group_len
    local_counts = lax.dynamic_slice_in_dim(counts, first_channel, local_count, 0)
    inv_scale = 1.0 / (local_counts.astype(jnp.float32) * spectra_all)
    scaled = vis_local * inv_scale[:, None, None, None]
    placed = lax.dynamic_update_slice_in_dim(
        jnp.zeros((OUTCH, 2, scaled.shape[2], INPUTS), jnp.float32), scaled, first_channel, 0
    )
    visibilities = lax.psum_scatter(
        placed.astype(jnp.bfloat16), "tm", scatter_dimension=3, tiled=True
    ).astype(jnp.float32)
    return (visibilities, beam_power)


def solution(mesh):
    return jax.shard_map(
        on_device,
        mesh=mesh,
        in_specs=(P(None, "stn", "tm", None), P(), P("stn"), P(), P()),
        out_specs=(P(None, None, "stn", "tm"), P("stn", "tm")),
        check_vma=False,
    )
```

profile of v0, /device:TPU:0, one launch (start us, length us, event | category | flops | bytes accessed | tf_op | source)
XLA Modules:
  0.0 849.8 jit_solution(14004677124410322033)
XLA Ops:
  7.3 28.2 %copy.75 = bf16[2,256,1,20736]{1,3,0,2:T(8,128)(2,1)} copy(bf16[2,256,1,20736]{3,1,2,0:T(8,128)(2,1)} %param.5) | data formatting | bytes 42467328 | tf_op args[0]
  35.5 17.1 %fusion = f32[2,256,3456]{1,2,0:T(8,128)} fusion(bf16[2,256,1,6,3456]{1,4,3,0,2:T(8,128)(2,1)} %bitcast.109, f32[6,3456]{1,0:T(8,128)S(1)} %copy-done.8), kind=kLoop, calls=%fused_computation.1 | loop fusion | flops 30081024 | bytes 28394496 | tf_op jit(solution)/shard_map/reduce_sum | solution.py:25
  52.6 6.4 fusion.122
  59.1 5.4 copy.77
  64.5 6.1 fusion.63
  70.6 5.6 copy.76
  76.3 4.4 fusion.65
  83.3 3.5 fusion.11
  86.8 3.7 fusion.18
  90.5 5.6 fusion.16
  96.1 3.8 add_bitcast_fusion
  99.8 5.5 copy.82
  105.3 9.3 %copy.86 = f32[1,256,1,3456]{3,1,2,0:T(8,128)} copy(f32[1,256,1,3456]{1,0,3,2:T(1,128)} %bitcast.115) | data formatting | bytes 7077888 | tf_op jit(solution)/shard_map/stack | solution.py:48
  114.6 6.9 subtract_bitcast_fusion
  121.5 5.4 copy.85
  126.9 8.9 %copy.87 = f32[1,256,1,3456]{3,1,2,0:T(8,128)} copy(f32[1,256,1,3456]{1,0,3,2:T(1,128)} %bitcast.116) | data formatting | bytes 7077888 | tf_op jit(solution)/shard_map/stack | solution.py:48
  135.8 5.4 fusion.9
  141.3 9.8 %copy.88 = bf16[2,256,1,3456]{1,0,2,3:T(2,128)(2,1)} copy(bf16[2,256,1,3456]{3,1,2,0:T(8,128)(2,1)} %fusion.9) | data formatting | bytes 7077888 | tf_op jit(solution)/shard_map/convert_element_type | solution.py:56
  151.1 86.8 %all_to_all.15 = bf16[2,256,1,3456]{1,0,2,3:T(2,128)(2,1)S(1)} all-to-all(bf16[2,256,1,3456]{1,0,2,3:T(2,128)(2,1)} %copy.88), channel_id=1, replica_groups=mesh['stn'=4,'tm'=8] {'tm'}, dimensions={3} | all-to-all | bytes 7077888 | tf_op jit(solution)/shard_map/all_to_all | solution.py:85
  242.4 122.2 %cosine_convert_fusion = (bf16[1,64,256,432]{2,1,0,3:T(8,128)(2,1)}, bf16[1,64,256,432]{2,1,0,3:T(8,128)(2,1)}) fusion(s32[432]{0:T(512)S(1)} %iota_add_fusion, s32[64,256]{1,0:T(8,128)S(1)} %constant_dynamic-slice_fusion), kind=kLoop, calls=%fused_computation.10 | loop fusion | flops 77856768 | bytes 28378816 | tf_op jit(solution)/shard_map/convert.5
  364.7 27.3 %fusion.24 = f32[2,2,64,8,432]{2,3,0,1,4:T(8,128)} fusion(bf16[1,64,256,432]{2,1,0,3:T(8,128)(2,1)} %get-tuple-element.15, bf16[1,64,256,432]{2,1,0,3:T(8,128)(2,1)} %get-tuple-element.14, bf16[2,256,8,432,1]{1,3,2,0,4:T(8,128)(2,1)S(1)} %bitcast.114), kind=kOutput, calls=%fused_computation.40 | convolution fusion | flops 509607936 | bytes 35389440 | tf_op jit(solution)/shard_map/pbik,qitk->pqbtk/dot_general | solution.py:63
  396.8 3.1 copy.95
  400.0 9.2 %all_to_all.12 = bf16[512,8,2,216]{0,3,2,1:T(8,128)(2,1)} reshape(bf16[2,256,1,3456]{1,0,2,3:T(2,128)(2,1)} %copy-done.4) | data formatting | bytes 7077888 | tf_op jit(solution)/shard_map/all_to_all | solution.py:85
  409.2 26.5 %copy.90 = bf16[2,1024,8,432]{1,0,3,2:T(2,128)(2,1)} copy(bf16[2,1024,8,432]{1,3,2,0:T(8,128)(2,1)} %all-gather.2.cloned.1.call-done) | data formatting | bytes 28311552 | tf_op jit(solution)/shard_map/all_gather | solution.py:100
  435.7 23.7 %reshape.240 = bf16[2048,8,2,216]{0,3,2,1:T(8,128)(2,1)} reshape(bf16[2,1024,8,432]{1,0,3,2:T(2,128)(2,1)} %copy.90) | data formatting | bytes 28311552 | tf_op jit(solution)/shard_map/reshape | solution.py:74
  459.4 12.3 %convolution_bitcast_fusion = f32[2,512,2048]{2,1,0:T(8,128)S(1)} fusion(bf16[2048,8,2,216]{0,3,2,1:T(8,128)(2,1)} %reshape.240, bf16[512,8,2,216]{0,3,2,1:T(8,128)(2,1)} %all_to_all.12, bf16[2,216]{1,0:T(2,128)(2,1)S(1)} %mul.249), kind=kOutput, calls=%fused_computation.17 | convolution fusion | flops 7249526784 | bytes 26084192 | tf_op jit(solution)/shard_map/atlg,btlg->lab/dot_general | solution.py:75
  472.7 6.0 broadcast_in_dim.2
  480.7 41.2 %copy.102 = bf16[16,2,256,1024]{2,1,0,3:T(2,128)(2,1)} copy(bf16[16,2,256,1024]{3,2,1,0:T(8,128)(2,1)} %copy_dynamic-update-slice_fusion) | data formatting | bytes 33554432
  521.9 27.6 %reshape.250 = bf16[1024,8192]{1,0:T(8,128)(2,1)} reshape(bf16[1024,16,2,256]{3,2,1,0:T(2,128)(2,1)} %bitcast.110) | data formatting | bytes 33554432
  551.7 279.4 %reduce-scatter.7.cloned.1.call-done = bf16[128,8192]{1,0:T(8,128)(2,1)} async-done(((bf16[1024,8192]{1,0:T(8,128)(2,1)}), bf16[128,8192]{1,0:T(8,128)(2,1)}) %reduce-scatter.7.cloned.1.call-update) | async-done | bytes 2097168
  831.0 4.5 reshape.251
  835.5 5.0 copy.103
  (52 shorter events, 19.7 us)
Async XLA Ops:
  7.2 235.3 %copy-start = (s32[64,1024]{1,0:T(8,128)S(1)}, s32[64,1024]{1,0:T(8,128)}, u32[]{:S(2)}) copy-start(s32[64,1024]{1,0:T(8,128)} %param.9) | copy-start | bytes 786436
  7.2 402.0 %all-gather.2.cloned.1.call-start = ((), (), s32[]{:S(2)}) async-start(), calls=%async_computation.3 | async-start | bytes 17694720 | tf_op jit(solution)/shard_map/all_gather | solution.py:100
  7.3 28.2 %copy-start.8 = (f32[6,3456]{1,0:T(8,128)S(1)}, f32[6,3456]{1,0:T(8,128)}, u32[]{:S(2)}) copy-start(f32[6,3456]{1,0:T(8,128)} %param.6) | copy-start | bytes 248836
  76.3 4.5 copy-start.3
  76.3 4.7 copy-start.6
  81.0 2.3 copy-start.2
  86.8 9.3 %copy-start.5 = (f32[256,27,128]{2,1,0:T(8,128)}, f32[256,27,128]{2,1,0:T(8,128)S(1)}, u32[]{:S(2)}) copy-start(f32[256,27,128]{2,1,0:T(8,128)S(1)} %get-tuple-element.8) | copy-start | bytes 10616836
  126.9 8.9 %copy-start.10 = (s32[256]{0:T(256)S(1)}, s32[256]{0:T(256)}, u32[]{:S(2)}) copy-start(s32[256]{0:T(256)} %param.7) | copy-start | bytes 3076
  237.8 1.8 copy-start.4
  239.6 2.4 copy-start.9
  241.9 307.7 %reduce-scatter.5.cloned.1.call-start = ((), (), s32[]{:S(2)}) async-start(), calls=%async_computation.4 | async-start | bytes 1310720 | tf_op jit(solution)/shard_map/reduce_scatter | solution.py:103
  242.4 122.2 %copy-start.7 = (bf16[2,256,1,3456]{1,3,0,2:T(8,128)(2,1)S(1)}, bf16[2,256,1,3456]{1,3,0,2:T(8,128)(2,1)}, u32[]{:S(2)}) copy-start(bf16[2,256,1,3456]{1,3,0,2:T(8,128)(2,1)} %copy.89) | copy-start | bytes 10616836
  400.0 431.1 %reduce-scatter.7.cloned.1.call-start = ((), (), s32[]{:S(2)}) async-start(), calls=%async_computation.5 | async-start | bytes 18874368
  835.5 7.5 copy-start.1
Sparse Core Ops, SparseCore 0:
  242.0 91.5 all-gather.1
  400.1 23.5 reduce-scatter.4
  549.7 281.3 reduce-scatter.6
where the time goes:
time: 858 us; the launch traced here: 850 us
  waiting for transfers between devices  279 us (33%)
  local copies, waits for them, and re-layouts  237 us (28%)
  other arithmetic  157 us (18%)
  blocking collectives  86.8 us (10%)
  matrix products  75.8 us (9%)
  between operations  14.2 us (2%)
    unnamed x4, waiting for transfers between devices  279 us
    another operation x1, other arithmetic  122 us
    unnamed x29, local copies, waits for them, and re-layouts  109 us
    all_to_all x1, blocking collectives, on_device(): lax.all_to_all(spectra, 'tm', split_axis=3, concat_axis=2, tiled=True)  86.8 us
    dot_general x1, matrix products, beam_terms(): jnp.einsum('pbik,qitk->pqbtk', weights, incoming, preferred_element_type=...  27.3 us
    all_gather x1, local copies, waits for them, and re-layouts, on_device(): lax.all_gather(turned, 'stn', axis=1, tiled=True)  26.5 us
    reshape x1, local copies, waits for them, and re-layouts, cross_products(): right_data.reshape(2 * col_count, spec_count, local_count, sub_len)  23.7 us
    another operation x2, local copies, waits for them, and re-layouts, fine_spectra(): jnp.stack([third_real.reshape(inputs_dev, spec_dev, FINE), third_imag.res...  18.2 us
  transfers between devices with their start and end apart: 3, of which 1 were waited for; matrix products, arithmetic and copies ran while one was open for 35% of the time, Pallas kernels for 0%

commit v1 on v0

--- a/solution.py
+++ b/solution.py
@@ -9,6 +9,27 @@
 OUTCH = 16
 TAPS = 6
 TRANSFORM_PRECISION = lax.Precision.HIGH
+
+
+def joined_along(blocks, dim):
+    blocks = jnp.moveaxis(blocks, 0, dim)
+    lengths = blocks.shape
+    return blocks.reshape(*lengths[:dim], lengths[dim] * lengths[dim + 1], *lengths[dim + 2 :])
+
+
+def collected_by_bits(x, axis):
+    size, position = (lax.axis_size(axis), lax.axis_index(axis))
+    blocks, apart = (x[None], 1)
+    while apart < size:
+        theirs = lax.ppermute(blocks, axis, [(i, i ^ apart) for i in range(size)])
+        low = position & apart == 0
+        blocks = jnp.concatenate([jnp.where(low, blocks, theirs), jnp.where(low, theirs, blocks)])
+        apart *= 2
+    return blocks
+
+
+def gather_by_bits(x, axis, dim):
+    return joined_along(collected_by_bits(x, axis), dim)
 
 
 def phase_table(row_count, col_count, modulus):
@@ -96,9 +117,7 @@
     keep_wide = keep_local.astype(jnp.bfloat16)
     fine_global = fine_start + jnp.arange(fine_dev, dtype=jnp.int32)
     masked = turned * keep_wide
-    vis_local = cross_products(
-        masked, lax.all_gather(turned, "stn", axis=1, tiled=True), local_count, sub_len
-    )
+    vis_local = cross_products(masked, gather_by_bits(turned, "stn", 1), local_count, sub_len)
     own_delays = lax.dynamic_slice_in_dim(beam_delay, stn_index * inputs_dev, inputs_dev, 1)
     voltages = lax.psum_scatter(
         beam_terms(own_delays, turned, fine_global).astype(jnp.bfloat16),

time: 858 us -> 890 us (1.037)
  other arithmetic: 157 us -> 172 us
  local copies, waits for them, and re-layouts: 237 us -> 246 us
    transpose x0 -> x1, local copies, waits for them, and re-layouts: none -> 34.1 us  [joined_along(): blocks = jnp.moveaxis(blocks, 0, dim)]
    all_gather x1 -> x0, local copies, waits for them, and re-layouts: 26.5 us -> none  [on_device(): lax.all_gather(turned, 'stn', axis=1, tiled=True)]
    reshape x1 -> x0, local copies, waits for them, and re-layouts: 23.7 us -> none  [cross_products(): right_data.reshape(2 * col_count, spec_count, local_count, sub_len)]
    another operation x2 -> x3, local copies, waits for them, and re-layouts: 11.1 us -> 34.7 us  [the longest x1 23.6 us: cross_products(): right_data.reshape(2 * col_count, spec_count, local_count, sub_len)]
    select_n x0 -> x2, other arithmetic: none -> 9.37 us  [collected_by_bits(): jnp.where(low, blocks, theirs)]
    unnamed x29 -> x33, local copies, waits for them, and re-layouts: 109 us -> 111 us
    unnamed x4 -> x3, waiting for transfers between devices: 279 us -> 278 us
  transfers between devices with their start and end apart: 3 -> 4, of which waited for: 1 -> 2; matrix products, arithmetic and copies ran while one was open for 35% -> 36% of each run, Pallas kernels for 0% -> 0%
where the time goes in v1:
time: 890 us; the launch traced here: 881 us
  waiting for transfers between devices  285 us (32%)
  local copies, waits for them, and re-layouts  246 us (28%)
  other arithmetic  172 us (19%)
  blocking collectives  86.9 us (10%)
  matrix products  75.7 us (9%)
  between operations  14.6 us (2%)
    unnamed x3, waiting for transfers between devices  278 us
    another operation x1, other arithmetic  122 us
    unnamed x33, local copies, waits for them, and re-layouts  111 us
    all_to_all x1, blocking collectives, on_device(): lax.all_to_all(spectra, 'tm', split_axis=3, concat_axis=2, tiled=True)  86.9 us
    transpose x1, local copies, waits for them, and re-layouts, joined_along(): blocks = jnp.moveaxis(blocks, 0, dim)  34.1 us
    dot_general x1, matrix products, beam_terms(): jnp.einsum('pbik,qitk->pqbtk', weights, incoming, preferred_element_type=...  27.3 us
    another operation x1, local copies, waits for them, and re-layouts, cross_products(): right_data.reshape(2 * col_count, spec_count, local_count, sub_len)  23.6 us
    another operation x2, local copies, waits for them, and re-layouts, fine_spectra(): jnp.stack([third_real.reshape(inputs_dev, spec_dev, FINE), third_imag.res...  18.2 us
  transfers between devices with their start and end apart: 4, of which 2 were waited for; matrix products, arithmetic and copies ran while one was open for 36% of the time, Pallas kernels for 0%

profile of v1, /device:TPU:0, one launch (start us, length us, event | category | flops | bytes accessed | tf_op | source)
XLA Modules:
  0.0 881.1 jit_solution(2485124374473169535)
XLA Ops:
  7.3 28.3 %copy.78 = bf16[2,256,1,20736]{1,3,0,2:T(8,128)(2,1)} copy(bf16[2,256,1,20736]{3,1,2,0:T(8,128)(2,1)} %param.5) | data formatting | bytes 42467328 | tf_op args[0]
  35.6 17.1 %fusion = f32[2,256,3456]{1,2,0:T(8,128)} fusion(bf16[2,256,1,6,3456]{1,4,3,0,2:T(8,128)(2,1)} %bitcast.112, f32[6,3456]{1,0:T(8,128)S(1)} %copy-done.10), kind=kLoop, calls=%fused_computation.1 | loop fusion | flops 30081024 | bytes 28394496 | tf_op jit(solution)/shard_map/reduce_sum | solution.py:46
  52.8 6.4 fusion.122
  59.2 5.4 copy.80
  64.6 6.1 fusion.63
  70.7 5.7 copy.79
  76.4 4.4 fusion.65
  90.6 5.6 fusion.16
  96.2 3.8 add_bitcast_fusion
  100.0 5.5 copy.85
  105.5 9.3 %copy.89 = f32[1,256,1,3456]{3,1,2,0:T(8,128)} copy(f32[1,256,1,3456]{1,0,3,2:T(1,128)} %bitcast.117) | data formatting | bytes 7077888 | tf_op jit(solution)/shard_map/stack | solution.py:69
  114.8 6.9 subtract_bitcast_fusion
  121.7 5.4 copy.88
  127.1 8.9 %copy.90 = f32[1,256,1,3456]{3,1,2,0:T(8,128)} copy(f32[1,256,1,3456]{1,0,3,2:T(1,128)} %bitcast.118) | data formatting | bytes 7077888 | tf_op jit(solution)/shard_map/stack | solution.py:69
  136.0 5.4 fusion.9
  141.5 9.8 %copy.91 = bf16[2,256,1,3456]{1,0,2,3:T(2,128)(2,1)} copy(bf16[2,256,1,3456]{3,1,2,0:T(8,128)(2,1)} %fusion.9) | data formatting | bytes 7077888 | tf_op jit(solution)/shard_map/convert_element_type | solution.py:77
  151.2 86.9 %all_to_all.15 = bf16[2,256,1,3456]{1,0,2,3:T(2,128)(2,1)S(1)} all-to-all(bf16[2,256,1,3456]{1,0,2,3:T(2,128)(2,1)} %copy.91), channel_id=1, replica_groups=mesh['stn'=4,'tm'=8] {'tm'}, dimensions={3} | all-to-all | bytes 7077888 | tf_op jit(solution)/shard_map/all_to_all | solution.py:106
  242.2 6.6 collective-permute-done
  252.3 3.9 pad_maximum_fusion
  259.4 122.0 %cosine_convert_fusion = (bf16[1,64,256,432]{2,1,0,3:T(8,128)(2,1)}, bf16[1,64,256,432]{2,1,0,3:T(8,128)(2,1)}) fusion(s32[432]{0:T(512)S(1)} %iota_add_fusion, s32[64,256]{1,0:T(8,128)S(1)} %constant_dynamic-slice_fusion), kind=kLoop, calls=%fused_computation.10 | loop fusion | flops 77856768 | bytes 28378816 | tf_op jit(solution)/shard_map/convert.5
  381.4 27.3 %fusion.24 = f32[2,2,64,8,432]{2,3,0,1,4:T(8,128)} fusion(bf16[1,64,256,432]{2,1,0,3:T(8,128)(2,1)} %get-tuple-element.19, bf16[1,64,256,432]{2,1,0,3:T(8,128)(2,1)} %get-tuple-element.18, bf16[2,256,8,432,1]{1,0,3,2,4:T(2,128)(2,1)S(1)} %bitcast.114), kind=kOutput, calls=%fused_computation.46 | convolution fusion | flops 509607936 | bytes 35389440 | tf_op jit(solution)/shard_map/pbik,qitk->pqbtk/dot_general | solution.py:84
  416.7 9.2 %all_to_all.12 = bf16[512,8,2,216]{0,3,2,1:T(8,128)(2,1)} reshape(bf16[2,256,1,3456]{1,0,2,3:T(2,128)(2,1)} %copy-done.4) | data formatting | bytes 7077888 | tf_op jit(solution)/shard_map/all_to_all | solution.py:106
  425.9 5.8 broadcast_select_fusion.1
  433.7 34.1 %copy.93 = bf16[2,4,256,8,432]{2,1,0,4,3:T(4,128)(2,1)} copy(bf16[2,4,256,8,432]{2,4,3,0,1:T(8,128)(2,1)S(1)} %maximum_bitcast_fusion.2) | data formatting | bytes 28311552 | tf_op jit(solution)/shard_map/transpose | solution.py:15
  467.8 23.6 %reshape_reshape.3 = bf16[2048,8,2,216]{0,3,2,1:T(8,128)(2,1)} reshape(bf16[2,4,256,8,432]{2,1,0,4,3:T(4,128)(2,1)} %copy.93) | data formatting | bytes 28311552 | tf_op jit(solution)/shard_map/reshape;reshape | solution.py:95
  491.3 12.3 %convolution_bitcast_fusion = f32[2,512,2048]{2,1,0:T(8,128)S(1)} fusion(bf16[2048,8,2,216]{0,3,2,1:T(8,128)(2,1)} %reshape_reshape.3, bf16[512,8,2,216]{0,3,2,1:T(8,128)(2,1)} %all_to_all.12, bf16[2,216]{1,0:T(2,128)(2,1)S(1)} %mul.249), kind=kOutput, calls=%fused_computation.21 | convolution fusion | flops 7249526784 | bytes 26084192 | tf_op jit(solution)/shard_map/atlg,btlg->lab/dot_general | solution.py:96
  504.6 6.0 broadcast_in_dim.4
  512.6 41.3 %copy.108 = bf16[16,2,256,1024]{2,1,0,3:T(2,128)(2,1)} copy(bf16[16,2,256,1024]{3,2,1,0:T(8,128)(2,1)} %copy_dynamic-update-slice_fusion) | data formatting | bytes 33554432
  553.9 27.7 %reshape.247 = bf16[1024,8192]{1,0:T(8,128)(2,1)} reshape(bf16[1024,16,2,256]{3,2,1,0:T(2,128)(2,1)} %bitcast.113) | data formatting | bytes 33554432
  583.7 278.3 %reduce-scatter.7.cloned.1.call-done = bf16[128,8192]{1,0:T(8,128)(2,1)} async-done(((bf16[1024,8192]{1,0:T(8,128)(2,1)}), bf16[128,8192]{1,0:T(8,128)(2,1)}) %reduce-scatter.7.cloned.1.call-update) | async-done | bytes 2097168
  862.1 4.5 reshape.248
  866.5 5.0 copy.109
  (61 shorter events, 38.1 us)
Async XLA Ops:
  7.2 252.2 %copy-start = (s32[64,1024]{1,0:T(8,128)S(1)}, s32[64,1024]{1,0:T(8,128)}, u32[]{:S(2)}) copy-start(s32[64,1024]{1,0:T(8,128)} %param.9) | copy-start | bytes 786436
  7.2 574.4 %reduce-scatter.5.cloned.1.call-start = ((), (), s32[]{:S(2)}) async-start(), calls=%async_computation.3 | async-start | bytes 1310720 | tf_op jit(solution)/shard_map/reduce_scatter | solution.py:122
  7.3 28.3 %copy-start.10 = (f32[6,3456]{1,0:T(8,128)S(1)}, f32[6,3456]{1,0:T(8,128)}, u32[]{:S(2)}) copy-start(f32[6,3456]{1,0:T(8,128)} %param.6) | copy-start | bytes 248836
  76.4 4.5 copy-start.3
  76.4 4.7 copy-start.9
  81.2 2.3 copy-start.2
  87.0 9.3 %copy-start.8 = (f32[256,27,128]{2,1,0:T(8,128)}, f32[256,27,128]{2,1,0:T(8,128)S(1)}, u32[]{:S(2)}) copy-start(f32[256,27,128]{2,1,0:T(8,128)S(1)} %get-tuple-element.10) | copy-start | bytes 10616836
  127.1 8.9 %copy-start.12 = (s32[256]{0:T(256)S(1)}, s32[256]{0:T(256)}, u32[]{:S(2)}) copy-start(s32[256]{0:T(256)} %param.7) | copy-start | bytes 3076
  238.2 1.8 copy-start.4
  242.2 6.6 collective-permute-start
  252.3 4.0 copy-start.6
  252.3 5.1 copy-start.7
  252.3 6.6 copy-start.11
  257.4 168.5 %collective-permute-start.1 = (bf16[2,2,256,8,432]{2,4,3,1,0:T(8,128)(2,1)}, bf16[2,2,256,8,432]{2,4,3,1,0:T(8,128)(2,1)}, u32[]{:S(2)}, u32[]{:S(2)}) collective-permute-start(bf16[2,2,256,8,432]{2,4,3,1,0:T(8,128)(2,1)} %pad_maximum_fusion), channel_id=1, source_target_pairs={{0,16},{8,24},{16,0},{24,8},{1,17},{9,25},{17,1},{25,9},{2,18},{10... | collective-permute-start | bytes 21233672 | tf_op jit(solution)/shard_map/ppermute | solution.py:24
  259.4 122.1 %copy-start.5 = (bf16[2,256,1,3456]{1,0,2,3:T(2,128)(2,1)S(1)}, bf16[2,256,1,3456]{1,0,2,3:T(2,128)(2,1)}, u32[]{:S(2)}) copy-start(bf16[2,256,1,3456]{1,0,2,3:T(2,128)(2,1)} %copy-done.4) | copy-start | bytes 10616836
  416.7 445.4 %reduce-scatter.7.cloned.1.call-start = ((), (), s32[]{:S(2)}) async-start(), calls=%async_computation.4 | async-start | bytes 18874368
  866.5 7.5 copy-start.1
Sparse Core Ops, SparseCore 0:
  416.8 22.5 reduce-scatter.4
  581.7 280.2 reduce-scatter.6
